TPU v7x, 256 devices: a whole 4x4x8 slice. The times are simulated.
256 devices in a mesh: depth: 32 (over y, z), rows: 8 (over x, core).
Axes of the slice: x: 4, y: 4, z: 8, core: 2. Of those that a mesh axis runs over, the one named last changes fastest.
Arguments:
- density_raw: bfloat16 [1024, 128, 1024], P('depth', 'rows'), may hold values from -6 to 6
- colour_raw: bfloat16 [3, 1024, 128, 1024], P(None, 'depth', 'rows'), may hold values from -6 to 6
- target: float32 [3, 128, 1024], P(None, 'rows'), may hold values from 0 to 1
- slab_rank: int32 [32], replicated, may hold values from 0 to 31, each once
Outputs:
- grad_density: float32 [1024, 128, 1024], P('depth', 'rows')
- grad_colour: float32 [3, 1024, 128, 1024], P(None, 'depth', 'rows')
Inputs may be any that keep to these rules, and one draw needn't show every extreme that they name: slab_rank is a permutation: every slab has its own position along the rays.
All inputs are finite; a program needn't handle non-finite values.
Results may differ from a plain program's by a relative error of at most 0.0003.
Values may be sent and summed in bfloat16 or wider, within the bound.
A program may use at most 128 MiB of HBM per device.

v0:
```python
import jax
import jax.numpy as jnp
from jax import lax
from jax.sharding import Mesh
from jax.sharding import PartitionSpec as P

DEPTH = ("depth_0", "depth_1")


optical_depth = 2.5
smooth_weight = 0.05


def padded_2(value, sides, width):
    edges = {}
    for axis, dim in sides:
        peers, length = (lax.axis_size(axis), value.shape[dim])
        up = [(i, (i + 1) % peers) for i in range(peers - 1)]
        last = lax.slice_in_dim(value, length - width, length, axis=dim)
        initial = lax.slice_in_dim(value, 0, width, axis=dim)
        edges[dim] = (
            lax.ppermute(last, axis, up),
            lax.ppermute(initial, axis, [(b, a) for a, b in up]),
        )
    done = []
    for _, dim in sides:
        low, high = edges[dim]
        around = [(width, width) if d in done else (0, 0) for d in range(value.ndim)]
        value = jnp.concatenate([jnp.pad(low, around), value, jnp.pad(high, around)], axis=dim)
        done.append(dim)
    return value


def cut_along(value, dim, peers):
    shape = value.shape
    parts = value.reshape(*shape[:dim], peers, shape[dim] // peers, *shape[dim + 1 :])
    return jnp.moveaxis(parts, dim, 0)


def joined_along(parts, dim):
    shape = list(parts.shape[1:])
    shape[dim] *= parts.shape[0]
    return jnp.moveaxis(parts, 0, dim).reshape(shape)


def moved_by_axis(parts, axes, sequence):
    inside = parts.shape[1:]
    filled = parts.reshape(*(lax.axis_size(a) for a in axes), *inside)
    for k in sequence:
        filled = lax.all_to_all(filled, axes[k], k, k, tiled=True)
    return filled.reshape(-1, *inside)


def exchange_by_axis(value, axes, sequence, split_dim, concat_dim):
    parts = cut_along(value, split_dim, lax.axis_size(axes))
    return joined_along(moved_by_axis(parts, axes, sequence), concat_dim)


def along_rays(matrix, values):
    shape = values.shape
    flat = values.reshape(shape[0], shape[1], -1)
    mixed = jnp.einsum("ij,cjp->cip", matrix, flat, precision=lax.Precision.HIGHEST)
    return mixed.reshape(shape)


def triangles(count):
    index = jnp.arange(count, dtype=jnp.int32)
    before = (index[None, :] < index[:, None]).astype(jnp.float32)
    after = (index[None, :] > index[:, None]).astype(jnp.float32)
    return (before, after)


def slab_terms(density, colour_raw, step_depth):
    dense = density.astype(jnp.float32)
    colour = jax.nn.sigmoid(colour_raw.astype(jnp.float32))
    depth_term = step_depth * jax.nn.softplus(dense)
    opacity = -jnp.expm1(-depth_term)
    kept = jnp.exp(-depth_term)
    before, after = triangles(dense.shape[0])
    front_light = jnp.exp(-along_rays(before, depth_term[None]))[0]
    through = front_light * kept
    passing = jnp.exp(-jnp.sum(depth_term, axis=0))
    weighted = front_light[None] * opacity[None] * colour
    behind_local = along_rays(after, weighted) / through[None]
    after_light = passing[None] / through
    partial_value = jnp.concatenate([jnp.sum(weighted, axis=1), passing[None]], axis=0)
    return (partial_value, (dense, colour, opacity, behind_local, after_light, front_light))


def slab_gradients(saved, scaled_residual, scaled_behind, slices_total):
    dense, colour, opacity, behind_local, after_light, front_light = saved
    lit = front_light * opacity
    grad_colour = slices_total * scaled_residual[:, None] * lit[None] * colour * (1.0 - colour)
    inner = (
        jnp.sum(scaled_residual[:, None] * (colour - behind_local), axis=0)
        - after_light * scaled_behind[None]
    )
    grad_density = optical_depth * front_light * (1.0 - opacity) * jax.nn.sigmoid(dense) * inner
    return (grad_density, grad_colour)


def composite(partials, slab_rank, target_piece):
    count = partials.shape[1]
    one_hot = (slab_rank[:, None] == jnp.arange(count, dtype=jnp.int32)[None]).astype(
        partials.dtype
    )
    ordered = jnp.einsum("sk,csl->ckl", one_hot, partials, precision=lax.Precision.HIGHEST)
    emitted, kept = (ordered[:3], ordered[3:])
    before, after = triangles(count)
    front = jnp.exp(along_rays(before, jnp.log(kept)))
    weighted = front * emitted
    behind = along_rays(after, weighted) / (front * kept)
    residual = jnp.sum(weighted, axis=1) - target_piece
    scaled_residual = front * residual[:, None]
    scaled_behind = front * jnp.sum(residual[:, None] * behind, axis=0, keepdims=True)
    stacked = jnp.concatenate([scaled_residual, scaled_behind], axis=0)
    return jnp.einsum("sk,ckl->csl", one_hot, stacked, precision=lax.Precision.HIGHEST)


def smooth_rims(density_raw, slices_dev, rows_dev):
    padded = padded_2(density_raw, ((DEPTH, 0), ("rows", 1)), 1).astype(jnp.float32)
    centre = padded[1:-1, 1:-1]
    slice_index = lax.axis_index(DEPTH) * slices_dev + jnp.arange(slices_dev, dtype=jnp.int32)
    row_index = lax.axis_index("rows") * rows_dev + jnp.arange(rows_dev, dtype=jnp.int32)
    last_slice = slices_dev * lax.axis_size(DEPTH) - 1
    last_row = rows_dev * lax.axis_size("rows") - 1
    below = jnp.where((slice_index > 0)[:, None, None], centre - padded[:-2, 1:-1], 0.0)
    above = jnp.where((slice_index < last_slice)[:, None, None], centre - padded[2:, 1:-1], 0.0)
    upper = jnp.where((row_index > 0)[None, :, None], centre - padded[1:-1, :-2], 0.0)
    lower = jnp.where((row_index < last_row)[None, :, None], centre - padded[1:-1, 2:], 0.0)
    return 2.0 * smooth_weight * (below + above + upper + lower)


def local(density_raw, colour_raw, target, slab_rank):
    slices_dev = density_raw.shape[0]
    rows_dev = density_raw.shape[1]
    width = density_raw.shape[2]
    depth_count = lax.axis_size(DEPTH)
    slices_total = slices_dev * depth_count
    partial_value, saved = slab_terms(density_raw, colour_raw, optical_depth / slices_total)
    pixels = rows_dev * width
    stacked = partial_value.reshape(4, 1, pixels)
    target_flat = target.reshape(3, pixels)
    position = lax.axis_index(DEPTH)
    piece = pixels // depth_count
    received = exchange_by_axis(stacked, DEPTH, (0, 1), 2, 1)
    start = position * piece
    target_piece = lax.dynamic_slice_in_dim(target_flat, start, piece, 1)
    answers = composite(received, slab_rank, target_piece)
    mine = lax.all_to_all(answers, DEPTH, split_axis=1, concat_axis=2, tiled=True)[:, 0]
    mine = mine.reshape(4, rows_dev, width)
    grad_density, grad_colour = slab_gradients(saved, mine[:3], mine[3], slices_total)
    grad_density = grad_density + smooth_rims(density_raw, slices_dev, rows_dev)
    return (grad_density, grad_colour)


def solution(mesh):
    torus = Mesh(mesh.devices.reshape(4, 8, mesh.shape["rows"]), ("depth_0", "depth_1", "rows"))
    in_specs = (P(DEPTH, "rows", None), P(None, DEPTH, "rows", None), P(None, "rows", None), P())
    out_specs = (P(DEPTH, "rows", None), P(None, DEPTH, "rows", None))
    return jax.shard_map(local, mesh=torus, in_specs=in_specs, out_specs=out_specs, check_vma=False)
```

profile of v0, /device:TPU:4, one launch (start us, length us, event | category | flops | bytes accessed | tf_op | source)
XLA Modules:
  0.0 103.1 jit_solution(15577373791022387768)
XLA Ops:
  0.6 2.4 %fusion.16 = f32[32,16,1024]{2,1,0:T(8,128)S(1)} fusion(bf16[32,16,1024]{2,1,0:T(8,128)(2,1)} %param.4), kind=kLoop, calls=%fused_computation.27 | loop fusion | flops 4194304 | bytes 3145728 | tf_op jit(solution)/shard_map/mul | solution.py:76
  3.1 1.2 %copy.21 = f32[4,8,16,1024]{3,1,2,0:T(8,128)S(1)} copy(f32[4,8,16,1024]{3,2,1,0:T(8,128)S(1)} %bitcast.88) | data formatting | bytes 4194304
  4.3 1.2 %fusion = f32[16384,32]{0,1:T(8,128)S(1)} fusion(f32[32,16384]{1,0:T(8,128)S(1)} %bitcast.86), kind=kOutput, calls=%fused_computation.1 | convolution fusion | flops 201851904 | bytes 4194304 | tf_op jit(solution)/shard_map/ij,cjp->cip/dot_general | solution.py:62
  5.5 1.2 %copy.22 = f32[4,8,16,1024]{3,2,1,0:T(8,128)S(1)} copy(f32[4,8,16,1024]{3,1,2,0:T(8,128)S(1)} %bitcast.87) | data formatting | bytes 4194304
  6.8 3.5 %bitcast_multiply_fusion = (f32[32,16,1024]{2,1,0:T(8,128)}, f32[32,16,1024]{2,1,0:T(8,128)S(1)}, f32[16,1024]{1,0:T(8,128)S(1)}) fusion(f32[4,8,16,1024]{3,2,1,0:T(8,128)S(1)} %copy.22, bf16[32,16,1024]{2,1,0:T(8,128)(2,1)S(1)} %copy-done), kind=kLoop, calls=%fused_computation.28 | loop fusion | flops 6799360 | bytes 7405568 | tf_op jit(solution)/shard_map/mul | solution.py:81
  10.3 3.6 %fusion.58 = (f32[3,16,1024]{2,1,0:T(8,128)S(1)}, f32[3,32,16,1024]{3,2,1,0:T(8,128)}) fusion(bf16[3,32,16,1024]{3,2,1,0:T(8,128)(2,1)S(1)} %copy-done.6, f32[32,16,1024]{2,1,0:T(8,128)S(1)} %get-tuple-element.7), kind=kLoop, calls=%fused_computation.91 | loop fusion | flops 9388032 | bytes 11730944 | tf_op jit(solution)/shard_map/reduce_sum | solution.py:86
  13.9 0.7 copy.13
  14.7 4.5 %all-to-all-start = ((f32[4,8,4,1,512]{4,1,2,3,0:T(8,128)}), f32[4,8,4,1,512]{4,1,2,3,0:T(8,128)S(1)}, u32[]{:S(2)}, u32[]{:S(2)}) async-start(f32[4,8,4,1,512]{4,1,2,3,0:T(8,128)} %copy.13), calls=%async_computation | async-start | bytes 524288 | tf_op jit(solution)/shard_map/all_to_all | solution.py:50
  19.1 0.2 fusion.60
  19.4 1.9 %collective-permute-start = (bf16[32,1,1024]{2,1,0:T(2,128)(2,1)S(1)}, bf16[32,1,1024]{2,1,0:T(2,128)(2,1)S(1)}, u32[]{:S(2)}, u32[]{:S(2)}) collective-permute-start(bf16[32,1,1024]{2,1,0:T(2,128)(2,1)S(1)} %get-tuple-element.11), channel_id=1, source_target_pairs={{0,1},{1,2},{2,3},{3,4},{4,5},{5,6},{6,7},{8,9},{9,10},{10,11},{11... | collective-permute-start | bytes 196616 | tf_op jit(solution)/shard_map/ppermute | solution.py:22
  21.3 3.6 %collective-permute-start.3 = (bf16[32,1,1024]{2,1,0:T(2,128)(2,1)S(1)}, bf16[32,1,1024]{2,1,0:T(2,128)(2,1)}, u32[]{:S(2)}, u32[]{:S(2)}) collective-permute-start(bf16[32,1,1024]{2,1,0:T(2,128)(2,1)S(1)} %get-tuple-element.12), channel_id=1, source_target_pairs={{1,0},{2,1},{3,2},{4,3},{5,4},{6,5},{7,6},{9,8},{10,9},{11,10},{12... | collective-permute-start | bytes 196616 | tf_op jit(solution)/shard_map/ppermute | solution.py:23
  24.9 3.8 %collective-permute-start.1 = (bf16[1,16,1024]{2,1,0:T(8,128)(2,1)S(1)}, bf16[1,16,1024]{2,1,0:T(8,128)(2,1)S(1)}, u32[]{:S(2)}, u32[]{:S(2)}) collective-permute-start(bf16[1,16,1024]{2,1,0:T(8,128)(2,1)S(1)} %get-tuple-element.9), channel_id=1, source_target_pairs={{0,8},{8,16},{16,24},{24,32},{32,40},{40,48},{48,56},{56,64},{64,7... | collective-permute-start | bytes 98312 | tf_op jit(solution)/shard_map/ppermute | solution.py:22
  28.8 1.3 %collective-permute-start.2 = (bf16[1,16,1024]{2,1,0:T(8,128)(2,1)S(1)}, bf16[1,16,1024]{2,1,0:T(8,128)(2,1)S(1)}, u32[]{:S(2)}, u32[]{:S(2)}) collective-permute-start(bf16[1,16,1024]{2,1,0:T(8,128)(2,1)S(1)} %get-tuple-element.10), channel_id=1, source_target_pairs={{8,0},{16,8},{24,16},{32,24},{40,32},{48,40},{56,48},{64,56},{72,6... | collective-permute-start | bytes 98312 | tf_op jit(solution)/shard_map/ppermute | solution.py:23
  30.2 7.2 %reshape.109 = f32[3,32,16384]{2,1,0:T(8,128)} reshape(f32[3,32,16,1024]{3,2,1,0:T(8,128)} %get-tuple-element.3) | data formatting | bytes 12582912 | tf_op jit(solution)/shard_map/reshape | solution.py:61
  37.4 0.9 copy.14
  38.3 10.4 %all-to-all-start.1 = ((f32[4,8,4,1,512]{4,0,2,3,1:T(4,128)}), f32[4,8,4,1,512]{4,0,2,3,1:T(4,128)S(1)}, u32[]{:S(2)}, u32[]{:S(2)}) async-start(f32[4,8,4,1,512]{4,0,2,3,1:T(4,128)} %copy.14), calls=%async_computation.1 | async-start | bytes 524288 | tf_op jit(solution)/shard_map/all_to_all | solution.py:50
  48.7 8.6 %fusion.47 = f32[3,16384,32]{1,2,0:T(8,128)} fusion(f32[3,32,16384]{2,1,0:T(8,128)} %reshape.109), kind=kOutput, calls=%fused_computation.79 | convolution fusion | flops 603980800 | bytes 12582912 | tf_op jit(solution)/shard_map/ij,cjp->cip/dot_general | solution.py:62
  57.3 2.4 %all-to-all-done.1 = f32[4,8,4,1,512]{4,0,2,3,1:T(4,128)S(1)} async-done(((f32[4,8,4,1,512]{4,0,2,3,1:T(4,128)}), f32[4,8,4,1,512]{4,0,2,3,1:T(4,128)S(1)}, u32[]{:S(2)}, u32[]{:S(2)}) %all-to-all-start.1) | async-done | bytes 262176 | tf_op jit(solution)/shard_map/all_to_all | solution.py:50
  59.8 0.5 convolution_bitcast_fusion.1
  60.5 0.2 fusion.31
  60.8 0.3 convolution_bitcast_fusion
  61.1 0.9 copy.17
  62.0 8.3 %all-to-all-start.2 = ((f32[4,32,512]{2,0,1:T(4,128)}), f32[4,32,512]{2,0,1:T(4,128)}, u32[]{:S(2)}, u32[]{:S(2)}) async-start(f32[4,32,512]{2,0,1:T(4,128)} %copy.17), calls=%async_computation.2 | async-start | bytes 524288 | tf_op jit(solution)/shard_map/all_to_all | solution.py:150
  70.3 10.2 %copy.24 = f32[12,8,16,1024]{3,2,1,0:T(8,128)} copy(f32[12,8,16,1024]{3,1,2,0:T(8,128)} %bitcast.84) | data formatting | bytes 12582912
  80.6 1.7 %fusion.27 = f32[34,18,1024]{2,1,0:T(8,128)S(1)} fusion(bf16[32,1,1024]{2,1,0:T(2,128)(2,1)} %collective-permute-done.3, bf16[32,1,1024]{2,1,0:T(2,128)(2,1)S(1)} %collective-permute-done, bf16[1,16,1024]{2,1,0:T(8,128)(2,1)S(1)} %collective-permute-done.2, bf16[32,16,1024]{2,1,0:T(8,128)(2,1)S(1)} %copy-done.1, ...), kind=kLoop, calls=%fused_computation.46 | loop fusion | flops 8773632 | bytes 3751936 | tf_op jit(solution)/shard_map/convert_element_type | solution.py:121
  82.3 1.7 %copy.18 = f32[3,32,512]{2,1,0:T(8,128)} copy(f32[3,32,512]{2,0,1:T(4,128)} %bitcast.83) | data formatting | bytes 393216 | tf_op jit(solution)/shard_map/slice | solution.py:152
  84.0 1.0 mul.156
  85.0 0.7 broadcast_multiply_fusion.1
  85.7 1.8 %slice_reduce_fusion = f32[32,512]{1,0:T(8,128)} fusion(f32[4,32,512]{2,0,1:T(4,128)} %all-to-all-done.2), kind=kLoop, calls=%fused_computation.66 | loop fusion | bytes 131072 | tf_op jit(solution)/shard_map/slice | solution.py:152
  87.4 1.5 %mul.160 = f32[16,1024]{1,0:T(8,128)} reshape(f32[32,512]{1,0:T(8,128)} %slice_reduce_fusion) | data formatting | bytes 131072 | tf_op jit(solution)/shard_map/mul | solution.py:96
  88.9 8.4 %subtract_multiply_fusion = (f32[3,32,16,1024]{3,2,1,0:T(8,128)}, f32[32,16,1024]{2,1,0:T(8,128)S(1)}) fusion(f32[3,16,1024]{2,1,0:T(8,128)} %broadcast_multiply_fusion.1, f32[32,16,1024]{2,1,0:T(8,128)} %copy-done.5, bf16[3,32,16,1024]{3,2,1,0:T(8,128)(2,1)} %param.5, f32[32,16,1024]{2,1,0:T(8,128)} %get-tuple-element.6, f32[3,16,1024]{2,1,0:T(8,128)S(1)} %mul.156, ...), kind=kLoop, calls=%fused_computation.5 | loop fusion | flops 18350080 | bytes 22413312 | tf_op jit(solution)/shard_map/mul | solution.py:93
  97.4 5.7 %fusion.11 = f32[32,16,1024]{2,1,0:T(8,128)} fusion(bf16[32,16,1024]{2,1,0:T(8,128)(2,1)S(1)} %copy-done.2, f32[4,8,16,1024]{3,2,1,0:T(8,128)S(1)} %copy-done.4, f32[34,18,1024]{2,1,0:T(8,128)S(1)} %fusion.27, f32[32,16,1024]{2,1,0:T(8,128)S(1)} %get-tuple-element.5, f32[16,1024]{1,0:T(8,128)S(1)} %copy-done.9, f32[16,1024]{1,0:T(8,128)S(1)} %copy-done.8, ...), kind=kLoop, calls=%fused_computation.22 | loop fusion | flops 18350080 | bytes 17956960 | tf_op jit(solution)/shard_map/add | solution.py:153
  (44 shorter events, 0.6 us)
Async XLA Ops:
  5.5 1.2 %copy-start = (bf16[32,16,1024]{2,1,0:T(8,128)(2,1)S(1)}, bf16[32,16,1024]{2,1,0:T(8,128)(2,1)}, u32[]{:S(2)}) copy-start(bf16[32,16,1024]{2,1,0:T(8,128)(2,1)} %param.4) | copy-start | bytes 3145732
  6.8 3.5 %copy-start.3 = (f32[4,8,16,1024]{3,2,1,0:T(8,128)}, f32[4,8,16,1024]{3,2,1,0:T(8,128)S(1)}, u32[]{:S(2)}) copy-start(f32[4,8,16,1024]{3,2,1,0:T(8,128)S(1)} %copy.22) | copy-start | bytes 6291460
  6.8 3.5 %copy-start.6 = (bf16[3,32,16,1024]{3,2,1,0:T(8,128)(2,1)S(1)}, bf16[3,32,16,1024]{3,2,1,0:T(8,128)(2,1)}, u32[]{:S(2)}) copy-start(bf16[3,32,16,1024]{3,2,1,0:T(8,128)(2,1)} %param.5) | copy-start | bytes 9437188
  10.2 3.6 %copy-start.5 = (f32[32,16,1024]{2,1,0:T(8,128)}, f32[32,16,1024]{2,1,0:T(8,128)S(1)}, u32[]{:S(2)}) copy-start(f32[32,16,1024]{2,1,0:T(8,128)S(1)} %get-tuple-element.7) | copy-start | bytes 6291460
  13.8 16.3 %copy-start.10 = (f32[3,16,1024]{2,1,0:T(8,128)S(1)}, f32[3,16,1024]{2,1,0:T(8,128)}, u32[]{:S(2)}) copy-start(f32[3,16,1024]{2,1,0:T(8,128)} %param.6) | copy-start | bytes 589828
  13.9 0.8 copy-start.7
  14.7 22.7 %all-to-all-start = ((f32[4,8,4,1,512]{4,1,2,3,0:T(8,128)}), f32[4,8,4,1,512]{4,1,2,3,0:T(8,128)S(1)}, u32[]{:S(2)}, u32[]{:S(2)}) async-start(f32[4,8,4,1,512]{4,1,2,3,0:T(8,128)} %copy.13), calls=%async_computation | async-start | bytes 524288 | tf_op jit(solution)/shard_map/all_to_all | solution.py:50
  19.4 61.2 %collective-permute-start = (bf16[32,1,1024]{2,1,0:T(2,128)(2,1)S(1)}, bf16[32,1,1024]{2,1,0:T(2,128)(2,1)S(1)}, u32[]{:S(2)}, u32[]{:S(2)}) collective-permute-start(bf16[32,1,1024]{2,1,0:T(2,128)(2,1)S(1)} %get-tuple-element.11), channel_id=1, source_target_pairs={{0,1},{1,2},{2,3},{3,4},{4,5},{5,6},{6,7},{8,9},{9,10},{10,11},{11... | collective-permute-start | bytes 196616 | tf_op jit(solution)/shard_map/ppermute | solution.py:22
  21.3 59.3 %collective-permute-start.3 = (bf16[32,1,1024]{2,1,0:T(2,128)(2,1)S(1)}, bf16[32,1,1024]{2,1,0:T(2,128)(2,1)}, u32[]{:S(2)}, u32[]{:S(2)}) collective-permute-start(bf16[32,1,1024]{2,1,0:T(2,128)(2,1)S(1)} %get-tuple-element.12), channel_id=1, source_target_pairs={{1,0},{2,1},{3,2},{4,3},{5,4},{6,5},{7,6},{9,8},{10,9},{11,10},{12... | collective-permute-start | bytes 196616 | tf_op jit(solution)/shard_map/ppermute | solution.py:23
  24.9 55.6 %collective-permute-start.1 = (bf16[1,16,1024]{2,1,0:T(8,128)(2,1)S(1)}, bf16[1,16,1024]{2,1,0:T(8,128)(2,1)S(1)}, u32[]{:S(2)}, u32[]{:S(2)}) collective-permute-start(bf16[1,16,1024]{2,1,0:T(8,128)(2,1)S(1)} %get-tuple-element.9), channel_id=1, source_target_pairs={{0,8},{8,16},{16,24},{24,32},{32,40},{40,48},{48,56},{56,64},{64,7... | collective-permute-start | bytes 98312 | tf_op jit(solution)/shard_map/ppermute | solution.py:22
  28.8 51.8 %collective-permute-start.2 = (bf16[1,16,1024]{2,1,0:T(8,128)(2,1)S(1)}, bf16[1,16,1024]{2,1,0:T(8,128)(2,1)S(1)}, u32[]{:S(2)}, u32[]{:S(2)}) collective-permute-start(bf16[1,16,1024]{2,1,0:T(8,128)(2,1)S(1)} %get-tuple-element.10), channel_id=1, source_target_pairs={{8,0},{16,8},{24,16},{32,24},{40,32},{48,40},{56,48},{64,56},{72,6... | collective-permute-start | bytes 98312 | tf_op jit(solution)/shard_map/ppermute | solution.py:23
  38.3 21.5 %all-to-all-start.1 = ((f32[4,8,4,1,512]{4,0,2,3,1:T(4,128)}), f32[4,8,4,1,512]{4,0,2,3,1:T(4,128)S(1)}, u32[]{:S(2)}, u32[]{:S(2)}) async-start(f32[4,8,4,1,512]{4,0,2,3,1:T(4,128)} %copy.14), calls=%async_computation.1 | async-start | bytes 524288 | tf_op jit(solution)/shard_map/all_to_all | solution.py:50
  48.7 11.1 %copy-start.11 = (s32[32]{0:T(128)S(1)}, s32[32]{0:T(128)}, u32[]{:S(2)}) copy-start(s32[32]{0:T(128)} %param.7) | copy-start | bytes 388
  62.0 20.3 %all-to-all-start.2 = ((f32[4,32,512]{2,0,1:T(4,128)}), f32[4,32,512]{2,0,1:T(4,128)}, u32[]{:S(2)}, u32[]{:S(2)}) async-start(f32[4,32,512]{2,0,1:T(4,128)} %copy.17), calls=%async_computation.2 | async-start | bytes 524288 | tf_op jit(solution)/shard_map/all_to_all | solution.py:150
  70.3 10.3 %copy-start.1 = (bf16[32,16,1024]{2,1,0:T(8,128)(2,1)S(1)}, bf16[32,16,1024]{2,1,0:T(8,128)(2,1)}, u32[]{:S(2)}) copy-start(bf16[32,16,1024]{2,1,0:T(8,128)(2,1)} %param.4) | copy-start | bytes 3145732
  88.9 8.4 %copy-start.2 = (bf16[32,16,1024]{2,1,0:T(8,128)(2,1)S(1)}, bf16[32,16,1024]{2,1,0:T(8,128)(2,1)}, u32[]{:S(2)}) copy-start(bf16[32,16,1024]{2,1,0:T(8,128)(2,1)} %param.4) | copy-start | bytes 3145732
  88.9 8.4 %copy-start.4 = (f32[4,8,16,1024]{3,2,1,0:T(8,128)S(1)}, f32[4,8,16,1024]{3,2,1,0:T(8,128)}, u32[]{:S(2)}) copy-start(f32[4,8,16,1024]{3,2,1,0:T(8,128)} %copy-done.3) | copy-start | bytes 6291460
  88.9 8.4 %copy-start.8 = (f32[16,1024]{1,0:T(8,128)S(1)}, f32[16,1024]{1,0:T(8,128)}, u32[]{:S(2)}) copy-start(f32[16,1024]{1,0:T(8,128)} %copy-done.7) | copy-start | bytes 196612
  88.9 8.5 %copy-start.9 = (f32[16,1024]{1,0:T(8,128)S(1)}, f32[16,1024]{1,0:T(8,128)}, u32[]{:S(2)}) copy-start(f32[16,1024]{1,0:T(8,128)} %mul.160) | copy-start | bytes 196612
where the time goes:
time: 104 us; the launch traced here: 103 us
  starting transfers between devices  33.8 us (32%)
  local copies, waits for them, and re-layouts  28.7 us (28%)
  other arithmetic  26.1 us (25%)
  matrix products  11 us (11%)
  waiting for transfers between devices  2.46 us (2%)
    all_to_all x2, starting transfers between devices, moved_by_axis(): filled = lax.all_to_all(filled, axes[k], k, k, tiled=True)  14.9 us
    unnamed x28, local copies, waits for them, and re-layouts  12.9 us
    dot_general x4, matrix products, along_rays(): jnp.einsum('ij,cjp->cip', matrix, flat, precision=lax.Precision.HIGHEST)  10.2 us
    mul x2, other arithmetic, slab_gradients(): slices_total * scaled_residual[:, None] * lit[None] * colour  9.12 us
    all_to_all x1, starting transfers between devices, local(): lax.all_to_all(answers, DEPTH, split_axis=1, concat_axis=2, tiled=True)  8.25 us
    reshape x1, local copies, waits for them, and re-layouts, along_rays(): flat = values.reshape(shape[0], shape[1], -1)  7.16 us
    ppermute x2, starting transfers between devices, padded_2(): lax.ppermute(last, axis, up)  5.74 us
    add x1, other arithmetic, local(): grad_density = grad_density + smooth_rims(density_raw, slices_dev, rows_dev)  5.7 us
  transfers between devices with their start and end apart: 7, of which 1 were waited for; matrix products, arithmetic and copies ran while one was open for 30% of the time, Pallas kernels for 0%

commit v1 on v0

v1 whole, which is shorter than its diff:
```python
import functools

import jax
import jax.numpy as jnp
from jax import lax
from jax.experimental import pallas as pl
from jax.experimental.pallas import tpu as pltpu
from jax.sharding import PartitionSpec as P

optical_depth = 2.5
smooth_weight = 0.05

LANES = 128
BAND_ROWS = 4
UNROLL = 8


def remote(src, dst, send_sem, recv_sem, axis, peer):
    return pltpu.make_async_remote_copy(
        src_ref=src,
        dst_ref=dst,
        send_sem=send_sem,
        recv_sem=recv_sem,
        device_id={axis: peer},
        device_id_type=pl.DeviceIdType.MESH,
    )


def light_kernel(
    slabs,
    groups,
    dens_hbm,
    colour_hbm,
    target_hbm,
    rank_ref,
    colour_out,
    lit_out,
    through_out,
    slope_out,
    smooth_out,
    answer_out,
    dens,
    colour_in,
    target_in,
    edge,
    edge_sent,
    rim_got,
    rim,
    partial_sent,
    partial_got,
    answer_sent,
    answer_got,
    dens_sem,
    colour_sem,
    target_sem,
    send_sem,
    recv_sem,
    rim_send_sem,
    rim_recv_sem,
):
    depth_at = lax.axis_index("depth")
    rows_at = lax.axis_index("rows")
    slices, rows, width = dens_hbm.shape
    blocks = width // LANES
    bands = rows // BAND_ROWS
    message = 4 * BAND_ROWS
    slices_total = slices * slabs
    step_depth = optical_depth / slices_total
    first_block = lax.rem(depth_at // bands + blocks // 2, blocks)

    def lanes_of(block):
        return pl.ds(pl.multiple_of(block * LANES, LANES), LANES)

    def rows_of(slab):
        return pl.ds(pl.multiple_of(slab * message, message), message)

    def input_copies(block):
        lanes = lanes_of(block)
        return (
            pltpu.make_async_copy(
                dens_hbm.at[:, :, lanes], dens.at[pl.ds(1, slices), :, lanes], dens_sem.at[block]
            ),
            pltpu.make_async_copy(
                colour_hbm.at[:, :, :, lanes], colour_in.at[:, :, :, lanes], colour_sem.at[block]
            ),
        )

    def start_inputs(k, _):
        for copy in input_copies(lax.rem(first_block + k, blocks)):
            copy.start()
        return 0

    lax.fori_loop(0, blocks, start_inputs, 0)
    my_block = depth_at // bands
    target_copy = pltpu.make_async_copy(
        target_hbm.at[:, :, lanes_of(my_block)], target_in, target_sem
    )
    target_copy.start()

    barrier = pltpu.get_barrier_semaphore()

    def greet(j, _):
        pl.semaphore_signal(
            barrier,
            inc=1,
            device_id={"depth": lax.rem(depth_at + j, slabs)},
            device_id_type=pl.DeviceIdType.MESH,
        )
        return 0

    lax.fori_loop(1, slabs, greet, 0)
    rows_up = lax.rem(rows_at + 1, groups)
    rows_down = lax.rem(rows_at + groups - 1, groups)
    depth_up = lax.rem(depth_at + 1, slabs)
    depth_down = lax.rem(depth_at + slabs - 1, slabs)
    for peer in (rows_up, rows_down):
        pl.semaphore_signal(
            barrier, inc=1, device_id={"rows": peer}, device_id_type=pl.DeviceIdType.MESH
        )

    slice_up = remote(
        dens_hbm.at[slices - 1], dens.at[0], rim_send_sem.at[0], rim_recv_sem.at[0], "depth", depth_up
    )
    slice_down = remote(
        dens_hbm.at[0],
        dens.at[slices + 1],
        rim_send_sem.at[1],
        rim_recv_sem.at[1],
        "depth",
        depth_down,
    )
    row_up = remote(
        edge_sent.at[1], rim_got.at[0], rim_send_sem.at[2], rim_recv_sem.at[2], "rows", rows_up
    )
    row_down = remote(
        edge_sent.at[0], rim_got.at[1], rim_send_sem.at[3], rim_recv_sem.at[3], "rows", rows_down
    )

    def partial_copy(owner):
        return remote(
            partial_sent.at[rows_of(owner)],
            partial_got.at[rows_of(depth_at)],
            send_sem.at[0],
            recv_sem.at[0],
            "depth",
            owner,
        )

    def forward_block(k, _):
        block = lax.rem(first_block + k, blocks)
        lanes = lanes_of(block)
        for copy in input_copies(block):
            copy.wait()

        def forward_step(step, carry):
            total, light, *shine = carry
            firsts, lasts = ([], [])
            for u in range(UNROLL):
                z = step * UNROLL + u
                x = dens[z + 1, :, lanes].astype(jnp.float32)
                firsts.append(x[:1])
                lasts.append(x[rows - 1 :])
                d = step_depth * jnp.log(1.0 + jnp.exp(x))
                opacity = d * (1.0 - d * (0.5 - d * (1.0 / 6.0 - d * (1.0 / 24.0))))
                lit = light * opacity
                total = total + d
                light = light - lit
                lit_out[z, :, lanes] = lit
                through_out[z, :, lanes] = light
                for c in range(3):
                    raw = colour_in[c, z, :, lanes].astype(jnp.float32)
                    colour = 1.0 / (1.0 + jnp.exp(-raw))
                    colour_out[c, z, :, lanes] = colour
                    shine[c] = shine[c] + lit * colour
            chunk = pl.ds(pl.multiple_of(step * UNROLL, UNROLL), UNROLL)
            edge[0, chunk, lanes] = jnp.concatenate(firsts, axis=0)
            edge[1, chunk, lanes] = jnp.concatenate(lasts, axis=0)
            return (total, light, *shine)

        zero = jnp.zeros((rows, LANES), jnp.float32)
        total, _, *shine = lax.fori_loop(
            0, slices // UNROLL, forward_step, (zero, zero + 1.0, zero, zero, zero)
        )
        base = pl.multiple_of(block * (bands * message), bands * message)
        for g in range(bands):
            for c, value in enumerate((*shine, total)):
                partial_sent[pl.ds(base + g * message + c * BAND_ROWS, BAND_ROWS), :] = value[
                    g * BAND_ROWS : (g + 1) * BAND_ROWS
                ]

        @pl.when(k == 0)
        def _():
            pl.semaphore_wait(barrier, slabs + 1)
            slice_up.start()
            slice_down.start()

        for g in range(bands):
            owner = block * bands + lax.rem(depth_at + g, bands)

            @pl.when(owner != depth_at)
            def _():
                partial_copy(owner).start()

        return 0

    lax.fori_loop(0, blocks, forward_block, 0)
    partial_got[rows_of(depth_at), :] = partial_sent[rows_of(depth_at), :]
    edge_sent[...] = edge[...].astype(jnp.bfloat16)
    row_up.start()
    row_down.start()

    ranks_row = jnp.zeros((slabs, LANES), jnp.int32)
    ranks_column = jnp.zeros((slabs, LANES), jnp.int32)
    lane = lax.broadcasted_iota(jnp.int32, (slabs, LANES), 1)
    sub = lax.broadcasted_iota(jnp.int32, (slabs, LANES), 0)
    for s in range(slabs):
        rank = rank_ref[s]
        ranks_row = jnp.where(lane == s, rank, ranks_row)
        ranks_column = jnp.where(sub == s, rank, ranks_column)
    earlier = (ranks_row < ranks_column).astype(jnp.float32)[:, :slabs]
    onward = (ranks_row >= ranks_column).astype(jnp.float32)[:, :slabs]

    def slope_block(block, _):
        lanes = lanes_of(block)

        def slope_step(step, _):
            for u in range(UNROLL):
                z = step * UNROLL + u
                x = dens[z + 1, :, lanes].astype(jnp.float32)
                slope_out[z, :, lanes] = optical_depth / (1.0 + jnp.exp(-x))
            return 0

        return lax.fori_loop(0, slices // UNROLL, slope_step, 0)

    lax.fori_loop(0, blocks, slope_block, 0)
    target_copy.wait()

    others = pl.ds(0, (slabs - 1) * message)
    pltpu.make_async_copy(partial_got.at[others], partial_got.at[others], recv_sem.at[0]).wait()

    def gathered(c):
        return jnp.concatenate(
            [
                partial_got[pl.ds(c * BAND_ROWS + j, slabs, stride=message), :]
                for j in range(BAND_ROWS)
            ],
            axis=1,
        )

    def mixed(matrix, value):
        return jnp.dot(
            matrix,
            value,
            precision=lax.Precision.HIGHEST,
            preferred_element_type=jnp.float32,
        )

    front = jnp.exp(-mixed(earlier, gathered(3)))
    band_row = lax.rem(depth_at, bands) * BAND_ROWS
    glow = jnp.zeros_like(front)
    answers = []
    for c in range(3):
        weighted = front * gathered(c)
        goal = jnp.concatenate(
            [target_in[c, pl.ds(band_row + j, 1), :] for j in range(BAND_ROWS)], axis=1
        )
        residual = jnp.sum(weighted, axis=0, keepdims=True) - goal
        glow = glow + residual * weighted
        answers.append(front * residual)
    answers.append(mixed(onward, glow))
    for c, value in enumerate(answers):
        for j in range(BAND_ROWS):
            answer_sent[pl.ds(c * BAND_ROWS + j, slabs, stride=message), :] = value[
                :, j * LANES : (j + 1) * LANES
            ]

    def answer_copy(slab):
        return remote(
            answer_sent.at[rows_of(slab)],
            answer_got.at[rows_of(depth_at)],
            send_sem.at[1],
            recv_sem.at[1],
            "depth",
            slab,
        )

    def answer_start(j, _):
        answer_copy(lax.rem(depth_at + j + slabs // 2, slabs)).start()
        return 0

    lax.fori_loop(0, slabs // 2, answer_start, 0)
    lax.fori_loop(slabs // 2 + 1, slabs, answer_start, 0)
    answer_got[rows_of(depth_at), :] = answer_sent[rows_of(depth_at), :]

    for copy in (slice_up, slice_down, row_up, row_down):
        copy.wait()

    @pl.when(depth_at == 0)
    def _():
        dens[0] = dens[1]

    @pl.when(depth_at == slabs - 1)
    def _():
        dens[slices + 1] = dens[slices]

    rim[...] = rim_got[...].astype(jnp.float32)

    @pl.when(rows_at == 0)
    def _():
        rim[0] = edge[0]

    @pl.when(rows_at == groups - 1)
    def _():
        rim[1] = edge[1]

    def smooth_block(block, _):
        lanes = lanes_of(block)
        row = lax.broadcasted_iota(jnp.int32, (rows, LANES), 0)

        def smooth_step(step, carry):
            low, centre = carry
            chunk = pl.ds(pl.multiple_of(step * UNROLL, UNROLL), UNROLL)
            above, below = (rim[0, chunk, lanes], rim[1, chunk, lanes])
            for u in range(UNROLL):
                z = step * UNROLL + u
                high = dens[z + 2, :, lanes].astype(jnp.float32)
                upper = jnp.where(row == 0, above[u : u + 1], pltpu.roll(centre, 1, axis=0))
                lower = jnp.where(
                    row == rows - 1, below[u : u + 1], pltpu.roll(centre, rows - 1, axis=0)
                )
                smooth_out[z, :, lanes] = (2.0 * smooth_weight) * (
                    (centre - low) + (centre - high) + (centre - upper) + (centre - lower)
                )
                low, centre = centre, high
            return low, centre

        start = (dens[0, :, lanes].astype(jnp.float32), dens[1, :, lanes].astype(jnp.float32))
        lax.fori_loop(0, slices // UNROLL, smooth_step, start)
        return 0

    lax.fori_loop(0, blocks, smooth_block, 0)

    pltpu.make_async_copy(answer_got.at[others], answer_got.at[others], recv_sem.at[1]).wait()
    answer_out[...] = answer_got[...]
    pltpu.make_async_copy(partial_sent.at[others], partial_sent.at[others], send_sem.at[0]).wait()
    pltpu.make_async_copy(answer_sent.at[others], answer_sent.at[others], send_sem.at[1]).wait()


def gradient_kernel(
    slices_total,
    colour_ref,
    lit_ref,
    through_ref,
    slope_ref,
    smooth_ref,
    answer_ref,
    dens_grad_hbm,
    colour_grad_hbm,
    dens_grad,
    colour_grad,
    dens_sem,
    colour_sem,
):
    slices, rows, width = lit_ref.shape
    blocks = width // LANES
    bands = rows // BAND_ROWS
    message = 4 * BAND_ROWS

    def output_copies(block):
        lanes = pl.ds(pl.multiple_of(block * LANES, LANES), LANES)
        return (
            pltpu.make_async_copy(
                dens_grad.at[:, :, lanes], dens_grad_hbm.at[:, :, lanes], dens_sem.at[block]
            ),
            pltpu.make_async_copy(
                colour_grad.at[:, :, :, lanes],
                colour_grad_hbm.at[:, :, :, lanes],
                colour_sem.at[block],
            ),
        )

    def gradient_block(block, _):
        lanes = pl.ds(pl.multiple_of(block * LANES, LANES), LANES)
        base = pl.multiple_of(block * (bands * message), bands * message)

        def answer(c):
            return jnp.concatenate(
                [
                    answer_ref[pl.ds(base + g * message + c * BAND_ROWS, BAND_ROWS), :]
                    for g in range(bands)
                ],
                axis=0,
            )

        residual = [answer(c) for c in range(3)]
        strong = [slices_total * value for value in residual]

        def gradient_step(step, remaining):
            for u in range(UNROLL):
                z = step * UNROLL + u
                lit = lit_ref[z, :, lanes]
                seen = jnp.zeros_like(lit)
                for c in range(3):
                    colour = colour_ref[c, z, :, lanes]
                    seen = seen + residual[c] * colour
                    colour_grad[c, z, :, lanes] = (strong[c] * lit) * (colour * (1.0 - colour))
                remaining = remaining - lit * seen
                dens_grad[z, :, lanes] = (
                    slope_ref[z, :, lanes] * (through_ref[z, :, lanes] * seen - remaining)
                    + smooth_ref[z, :, lanes]
                )
            return remaining

        lax.fori_loop(0, slices // UNROLL, gradient_step, answer(3))
        for copy in output_copies(block):
            copy.start()
        return 0

    lax.fori_loop(0, blocks, gradient_block, 0)

    def finish(block, _):
        for copy in output_copies(block):
            copy.wait()
        return 0

    lax.fori_loop(0, blocks, finish, 0)


def local(slabs, groups, density_raw, colour_raw, target, slab_rank):
    slices, rows, width = density_raw.shape
    blocks = width // LANES
    message = 4 * BAND_ROWS
    voxels = (slices, rows, width)
    f32 = jnp.float32
    bf16 = jnp.bfloat16
    anywhere = pl.BlockSpec(memory_space=pl.ANY)
    vmem = pl.BlockSpec(memory_space=pltpu.VMEM)
    packet = pltpu.VMEM((slabs * message, LANES), f32)
    saved = pl.pallas_call(
        functools.partial(light_kernel, slabs, groups),
        out_shape=(
            pltpu.VMEM((3, *voxels), f32),
            pltpu.VMEM(voxels, f32),
            pltpu.VMEM(voxels, f32),
            pltpu.VMEM(voxels, f32),
            pltpu.VMEM(voxels, f32),
            packet,
        ),
        in_specs=[anywhere, anywhere, anywhere, pl.BlockSpec(memory_space=pltpu.SMEM)],
        out_specs=(vmem,) * 6,
        scratch_shapes=[
            pltpu.VMEM((slices + 2, rows, width), bf16),
            pltpu.VMEM((3, *voxels), bf16),
            pltpu.VMEM((3, rows, LANES), f32),
            pltpu.VMEM((2, slices, width), f32),
            pltpu.VMEM((2, slices, width), bf16),
            pltpu.VMEM((2, slices, width), bf16),
            pltpu.VMEM((2, slices, width), f32),
            packet,
            packet,
            packet,
            packet,
            pltpu.SemaphoreType.DMA((blocks,)),
            pltpu.SemaphoreType.DMA((blocks,)),
            pltpu.SemaphoreType.DMA,
            pltpu.SemaphoreType.DMA((2,)),
            pltpu.SemaphoreType.DMA((2,)),
            pltpu.SemaphoreType.DMA((4,)),
            pltpu.SemaphoreType.DMA((4,)),
        ],
        compiler_params=pltpu.CompilerParams(
            collective_id=0, has_side_effects=True, vmem_limit_bytes=40 * 2**20
        ),
        name="light",
    )(density_raw, colour_raw, target, slab_rank)
    return pl.pallas_call(
        functools.partial(gradient_kernel, float(slices * slabs)),
        out_shape=(
            jax.ShapeDtypeStruct(voxels, f32),
            jax.ShapeDtypeStruct((3, *voxels), f32),
        ),
        in_specs=[vmem] * 6,
        out_specs=(anywhere, anywhere),
        scratch_shapes=[
            pltpu.VMEM(voxels, f32),
            pltpu.VMEM((3, *voxels), f32),
            pltpu.SemaphoreType.DMA((blocks,)),
            pltpu.SemaphoreType.DMA((blocks,)),
        ],
        compiler_params=pltpu.CompilerParams(vmem_limit_bytes=16 * 2**20),
        name="gradient",
    )(*saved)


def solution(mesh):
    return jax.shard_map(
        functools.partial(local, mesh.shape["depth"], mesh.shape["rows"]),
        mesh=mesh,
        in_specs=(P("depth", "rows", None), P(None, "depth", "rows", None), P(None, "rows", None), P()),
        out_specs=(P("depth", "rows", None), P(None, "depth", "rows", None)),
        check_vma=False,
    )
```

time: 104 us -> 35.2 us (0.34)
  Pallas kernels: 0 us -> 34.5 us
  starting transfers between devices: 33.8 us -> 0 us
  local copies, waits for them, and re-layouts: 28.7 us -> 0 us
  other arithmetic: 26.1 us -> 0 us
  matrix products: 11 us -> 0 us
  waiting for transfers between devices: 2.46 us -> 0 us
    pallas_call x0 -> x2, Pallas kernels: none -> 34.5 us  [the longest x1 30.4 us: local(): pl.pallas_call(functools.partial(light_kernel, slabs, groups), out_shape=...]
    all_to_all x3 -> x0, starting transfers between devices: 23.1 us -> none  [the longest x2 14.9 us: moved_by_axis(): filled = lax.all_to_all(filled, axes[k], k, k, tiled=True)]
    mul x6 -> x0, other arithmetic: 15.1 us -> none  [the longest x2 9.12 us: slab_gradients(): slices_total * scaled_residual[:, None] * lit[None] * colour]
    unnamed x28 -> x0, local copies, waits for them, and re-layouts: 12.9 us -> none
    dot_general x6 -> x0, matrix products: 11 us -> none  [the longest x4 10.2 us: along_rays(): jnp.einsum('ij,cjp->cip', matrix, flat, precision=lax.Precision.HIGHEST)]
    ppermute x4 -> x0, starting transfers between devices: 10.7 us -> none  [the longest x2 5.74 us: padded_2(): lax.ppermute(last, axis, up)]
    reshape x2 -> x0, local copies, waits for them, and re-layouts: 7.89 us -> none  [the longest x1 7.16 us: along_rays(): flat = values.reshape(shape[0], shape[1], -1)]
    add x1 -> x0, other arithmetic: 5.7 us -> none  [local(): grad_density = grad_density + smooth_rims(density_raw, slices_dev, rows_dev)]
  transfers between devices with their start and end apart: 7 -> 0, of which waited for: 1 -> 0; matrix products, arithmetic and copies ran while one was open for 30% -> 0% of each run, Pallas kernels for 0% -> 0%
where the time goes in v1:
time: 35.2 us; the launch traced here: 35.1 us
  Pallas kernels  34.5 us (98%)
  between operations  0.64 us (2%)
    pallas_call x1, Pallas kernels, local(): pl.pallas_call(functools.partial(light_kernel, slabs, groups), out_shape=...  30.4 us
    pallas_call x1, Pallas kernels, local(): pl.pallas_call(functools.partial(gradient_kernel, float(slices * slabs)),...  4.09 us

profile of v1, /device:TPU:4, one launch (start us, length us, event | category | flops | bytes accessed | tf_op | source)
XLA Modules:
  0.0 35.1 jit_solution(9798696829378156074)
XLA Ops:
  0.6 30.4 %light.1 = (f32[3,32,16,1024]{3,2,1,0:T(8,128)S(1)}, f32[32,16,1024]{2,1,0:T(8,128)S(1)}, f32[32,16,1024]{2,1,0:T(8,128)S(1)}, f32[32,16,1024]{2,1,0:T(8,128)S(1...) custom-call(bf16[32,16,1024]{2,1,0:T(8,128)(2,1)} %dens_hbm.1, bf16[3,32,16,1024]{3,2,1,0:T(8,128)(2,1)} %colour_hbm.1, ...), custom_call_target="tpu_custom_call" | custom-call | tf_op jit(solution)/shard_map/light/pallas_call | solution.py:439
  31.0 4.1 %gradient.1 = (f32[32,16,1024]{2,1,0:T(8,128)}, f32[3,32,16,1024]{3,2,1,0:T(8,128)}) custom-call(f32[3,32,16,1024]{3,2,1,0:T(8,128)S(1)} %get-tuple-element.8.colour_ref, f32[32,16,1024]{2,1,0:T(8,128)S(1)} %get-tuple-element.9.lit_ref, f32[32,16,1024]{2,1,0:T(8,128)S(1)} %get-tuple-element.10.through_ref, f32[32,16,1024]{2,1,0:T(8,128)S(1)} %get-tuple-element.11.slope_ref, ...), custom_call_target="tpu_custom_call" | custom-call | tf_op jit(solution)/shard_map/gradient/pallas_call | solution.py:476

commit v2 on v1

--- a/solution.py
+++ b/solution.py
@@ -1,4 +1,5 @@
 import functools
+import math
 
 import jax
 import jax.numpy as jnp
@@ -13,6 +14,58 @@
 LANES = 128
 BAND_ROWS = 4
 UNROLL = 8
+RAW_LIMIT = 6.0
+CODE_TOP = 32767.0
+ANSWER_KNEE = 2.0**-10
+
+
+def log_code(least, most):
+    low, high = (math.log(least) - 1e-3, math.log(most) + 1e-3)
+    return (0.5 * (low + high), 2.0 * CODE_TOP / (high - low))
+
+
+def partial_codes(slices, slices_total):
+    soft = (math.log1p(math.exp(-RAW_LIMIT)), math.log1p(math.exp(RAW_LIMIT)))
+    span = optical_depth / slices_total * slices
+    blocked = [-math.expm1(-span * value) for value in soft]
+    colour = [1.0 / (1.0 + math.exp(sign * RAW_LIMIT)) for sign in (1, -1)]
+    return [log_code(*colour)] * 3 + [log_code(*blocked)]
+
+
+def answer_scales():
+    return [math.asinh(top / ANSWER_KNEE) / CODE_TOP for top in (1.001, 1.001, 1.001, 3.01)]
+
+
+def to_code(value):
+    kept = jnp.clip(value, -CODE_TOP, CODE_TOP)
+    return jnp.floor(kept + 0.5)
+
+
+def from_log_code(code, middle, scale):
+    return jnp.exp(code * (1.0 / scale) + middle)
+
+
+def to_answer_code(value, scale):
+    tall = jnp.abs(value) * (1.0 / ANSWER_KNEE)
+    code = jnp.log(tall + jnp.sqrt(tall * tall + 1.0)) * (1.0 / scale)
+    return to_code(jnp.where(value < 0.0, -code, code))
+
+
+def from_answer_code(code, scale):
+    grown = jnp.exp(code * scale)
+    return (0.5 * ANSWER_KNEE) * (grown - 1.0 / grown)
+
+
+def far_first(k, count):
+    return lax.rem(count // 2 + (2 * (k % 2) - 1) * ((k + 1) // 2) + count, count)
+
+
+def as_words(code):
+    return code.astype(jnp.int32).astype(jnp.int16)
+
+
+def as_floats(words):
+    return words.astype(jnp.int32).astype(jnp.float32)
 
 
 def remote(src, dst, send_sem, recv_sem, axis, peer):
@@ -38,6 +91,7 @@
     through_out,
     slope_out,
     smooth_out,
+    mean_out,
     answer_out,
     dens,
     colour_in,
@@ -50,6 +104,7 @@
     partial_got,
     answer_sent,
     answer_got,
+    codes,
     dens_sem,
     colour_sem,
     target_sem,
@@ -66,7 +121,9 @@
     message = 4 * BAND_ROWS
     slices_total = slices * slabs
     step_depth = optical_depth / slices_total
-    first_block = lax.rem(depth_at // bands + blocks // 2, blocks)
+    my_block = lax.rem(depth_at, blocks)
+    my_band = depth_at // blocks
+    codings = partial_codes(slices, slices_total)
 
     def lanes_of(block):
         return pl.ds(pl.multiple_of(block * LANES, LANES), LANES)
@@ -85,13 +142,18 @@
             ),
         )
 
+    def block_at(k):
+        return lax.rem(my_block + far_first(k, blocks), blocks)
+
+    def owner_at(block, g):
+        return lax.rem(my_band + far_first(g, bands), bands) * blocks + block
+
     def start_inputs(k, _):
-        for copy in input_copies(lax.rem(first_block + k, blocks)):
+        for copy in input_copies(block_at(k)):
             copy.start()
         return 0
 
     lax.fori_loop(0, blocks, start_inputs, 0)
-    my_block = depth_at // bands
     target_copy = pltpu.make_async_copy(
         target_hbm.at[:, :, lanes_of(my_block)], target_in, target_sem
     )
@@ -147,13 +209,13 @@
         )
 
     def forward_block(k, _):
-        block = lax.rem(first_block + k, blocks)
+        block = block_at(k)
         lanes = lanes_of(block)
         for copy in input_copies(block):
             copy.wait()
 
         def forward_step(step, carry):
-            total, light, *shine = carry
+            blocked, light, *shine = carry
             firsts, lasts = ([], [])
             for u in range(UNROLL):
                 z = step * UNROLL + u
@@ -163,7 +225,7 @@
                 d = step_depth * jnp.log(1.0 + jnp.exp(x))
                 opacity = d * (1.0 - d * (0.5 - d * (1.0 / 6.0 - d * (1.0 / 24.0))))
                 lit = light * opacity
-                total = total + d
+                blocked = blocked + lit
                 light = light - lit
                 lit_out[z, :, lanes] = lit
                 through_out[z, :, lanes] = light
@@ -175,18 +237,25 @@
             chunk = pl.ds(pl.multiple_of(step * UNROLL, UNROLL), UNROLL)
             edge[0, chunk, lanes] = jnp.concatenate(firsts, axis=0)
             edge[1, chunk, lanes] = jnp.concatenate(lasts, axis=0)
-            return (total, light, *shine)
+            return (blocked, light, *shine)
 
         zero = jnp.zeros((rows, LANES), jnp.float32)
-        total, _, *shine = lax.fori_loop(
+        blocked, light, *shine = lax.fori_loop(
             0, slices // UNROLL, forward_step, (zero, zero + 1.0, zero, zero, zero)
         )
-        base = pl.multiple_of(block * (bands * message), bands * message)
+        mean = [value / blocked for value in shine]
+        for c in range(3):
+            mean_out[c, :, lanes] = shine[c] + light * mean[c]
+        mean_out[3, :, lanes] = light
+        coded = [
+            to_code((jnp.log(value) - middle) * scale)
+            for value, (middle, scale) in zip((*mean, blocked), codings)
+        ]
         for g in range(bands):
-            for c, value in enumerate((*shine, total)):
-                partial_sent[pl.ds(base + g * message + c * BAND_ROWS, BAND_ROWS), :] = value[
-                    g * BAND_ROWS : (g + 1) * BAND_ROWS
-                ]
+            packed = [value[g * BAND_ROWS : (g + 1) * BAND_ROWS] for value in coded]
+            partial_sent[rows_of(g * blocks + block), :] = as_words(
+                jnp.concatenate(packed, axis=0)
+            )
 
         @pl.when(k == 0)
         def _():
@@ -195,7 +264,7 @@
             slice_down.start()
 
         for g in range(bands):
-            owner = block * bands + lax.rem(depth_at + g, bands)
+            owner = owner_at(block, g)
 
             @pl.when(owner != depth_at)
             def _():
@@ -218,7 +287,7 @@
         ranks_row = jnp.where(lane == s, rank, ranks_row)
         ranks_column = jnp.where(sub == s, rank, ranks_column)
     earlier = (ranks_row < ranks_column).astype(jnp.float32)[:, :slabs]
-    onward = (ranks_row >= ranks_column).astype(jnp.float32)[:, :slabs]
+    later = (ranks_row > ranks_column).astype(jnp.float32)[:, :slabs]
 
     def slope_block(block, _):
         lanes = lanes_of(block)
@@ -238,14 +307,17 @@
     others = pl.ds(0, (slabs - 1) * message)
     pltpu.make_async_copy(partial_got.at[others], partial_got.at[others], recv_sem.at[0]).wait()
 
+    codes[...] = as_floats(partial_got[...])
+
     def gathered(c):
-        return jnp.concatenate(
+        coded = jnp.concatenate(
             [
-                partial_got[pl.ds(c * BAND_ROWS + j, slabs, stride=message), :]
+                codes[pl.ds(c * BAND_ROWS + j, slabs, stride=message), :]
                 for j in range(BAND_ROWS)
             ],
             axis=1,
         )
+        return from_log_code(coded, *codings[c])
 
     def mixed(matrix, value):
         return jnp.dot(
@@ -255,24 +327,33 @@
             preferred_element_type=jnp.float32,
         )
 
-    front = jnp.exp(-mixed(earlier, gathered(3)))
-    band_row = lax.rem(depth_at, bands) * BAND_ROWS
+    blocked = gathered(3)
+    kept = 1.0 - blocked
+    front = jnp.exp(mixed(earlier, jnp.log(kept)))
+    arriving = front * blocked
     glow = jnp.zeros_like(front)
+    expected = jnp.zeros_like(front)
     answers = []
     for c in range(3):
-        weighted = front * gathered(c)
+        mean = gathered(c)
+        weighted = arriving * mean
         goal = jnp.concatenate(
-            [target_in[c, pl.ds(band_row + j, 1), :] for j in range(BAND_ROWS)], axis=1
+            [target_in[c, pl.ds(my_band * BAND_ROWS + j, 1), :] for j in range(BAND_ROWS)], axis=1
         )
         residual = jnp.sum(weighted, axis=0, keepdims=True) - goal
+        seen = front * residual
         glow = glow + residual * weighted
-        answers.append(front * residual)
-    answers.append(mixed(onward, glow))
+        expected = expected + seen * mean
+        answers.append(seen)
+    answers.append(mixed(later, glow) / kept - expected)
+    scales = answer_scales()
     for c, value in enumerate(answers):
+        coded = to_answer_code(value, scales[c])
         for j in range(BAND_ROWS):
-            answer_sent[pl.ds(c * BAND_ROWS + j, slabs, stride=message), :] = value[
+            codes[pl.ds(c * BAND_ROWS + j, slabs, stride=message), :] = coded[
                 :, j * LANES : (j + 1) * LANES
             ]
+    answer_sent[...] = as_words(codes[...])
 
     def answer_copy(slab):
         return remote(
@@ -284,12 +365,18 @@
             slab,
         )
 
-    def answer_start(j, _):
-        answer_copy(lax.rem(depth_at + j + slabs // 2, slabs)).start()
-        return 0
-
-    lax.fori_loop(0, slabs // 2, answer_start, 0)
-    lax.fori_loop(slabs // 2 + 1, slabs, answer_start, 0)
+    def answer_start(k, _):
+        block = block_at(k)
+        for g in range(bands):
+            slab = owner_at(block, g)
+
+            @pl.when(slab != depth_at)
+            def _():
+                answer_copy(slab).start()
+
+        return 0
+
+    lax.fori_loop(0, blocks, answer_start, 0)
     answer_got[rows_of(depth_at), :] = answer_sent[rows_of(depth_at), :]
 
     for copy in (slice_up, slice_down, row_up, row_down):
@@ -353,6 +440,7 @@
     through_ref,
     slope_ref,
     smooth_ref,
+    mean_ref,
     answer_ref,
     dens_grad_hbm,
     colour_grad_hbm,
@@ -365,6 +453,8 @@
     blocks = width // LANES
     bands = rows // BAND_ROWS
     message = 4 * BAND_ROWS
+    band_rows = blocks * message
+    scales = answer_scales()
 
     def output_copies(block):
         lanes = pl.ds(pl.multiple_of(block * LANES, LANES), LANES)
@@ -381,18 +471,19 @@
 
     def gradient_block(block, _):
         lanes = pl.ds(pl.multiple_of(block * LANES, LANES), LANES)
-        base = pl.multiple_of(block * (bands * message), bands * message)
+        words = [
+            as_floats(answer_ref[pl.ds(pl.multiple_of(g * band_rows + block * message, message), message), :])
+            for g in range(bands)
+        ]
 
         def answer(c):
-            return jnp.concatenate(
-                [
-                    answer_ref[pl.ds(base + g * message + c * BAND_ROWS, BAND_ROWS), :]
-                    for g in range(bands)
-                ],
-                axis=0,
-            )
+            coded = [value[c * BAND_ROWS : (c + 1) * BAND_ROWS] for value in words]
+            return from_answer_code(jnp.concatenate(coded, axis=0), scales[c])
 
         residual = [answer(c) for c in range(3)]
+        whole = mean_ref[3, :, lanes] * answer(3)
+        for c in range(3):
+            whole = whole + residual[c] * mean_ref[c, :, lanes]
         strong = [slices_total * value for value in residual]
 
         def gradient_step(step, remaining):
@@ -411,7 +502,7 @@
                 )
             return remaining
 
-        lax.fori_loop(0, slices // UNROLL, gradient_step, answer(3))
+        lax.fori_loop(0, slices // UNROLL, gradient_step, whole)
         for copy in output_copies(block):
             copy.start()
         return 0
@@ -435,7 +526,7 @@
     bf16 = jnp.bfloat16
     anywhere = pl.BlockSpec(memory_space=pl.ANY)
     vmem = pl.BlockSpec(memory_space=pltpu.VMEM)
-    packet = pltpu.VMEM((slabs * message, LANES), f32)
+    packet = pltpu.VMEM((slabs * message, LANES), jnp.int16)
     saved = pl.pallas_call(
         functools.partial(light_kernel, slabs, groups),
         out_shape=(
@@ -444,10 +535,11 @@
             pltpu.VMEM(voxels, f32),
             pltpu.VMEM(voxels, f32),
             pltpu.VMEM(voxels, f32),
+            pltpu.VMEM((4, rows, width), f32),
             packet,
         ),
         in_specs=[anywhere, anywhere, anywhere, pl.BlockSpec(memory_space=pltpu.SMEM)],
-        out_specs=(vmem,) * 6,
+        out_specs=(vmem,) * 7,
         scratch_shapes=[
             pltpu.VMEM((slices + 2, rows, width), bf16),
             pltpu.VMEM((3, *voxels), bf16),
@@ -460,6 +552,7 @@
             packet,
             packet,
             packet,
+            pltpu.VMEM((slabs * message, LANES), f32),
             pltpu.SemaphoreType.DMA((blocks,)),
             pltpu.SemaphoreType.DMA((blocks,)),
             pltpu.SemaphoreType.DMA,
@@ -479,7 +572,7 @@
             jax.ShapeDtypeStruct(voxels, f32),
             jax.ShapeDtypeStruct((3, *voxels), f32),
         ),
-        in_specs=[vmem] * 6,
+        in_specs=[vmem] * 7,
         out_specs=(anywhere, anywhere),
         scratch_shapes=[
             pltpu.VMEM(voxels, f32),

time: 35.2 us -> 30.1 us (0.86)
  Pallas kernels: 34.5 us -> 29.3 us
    pallas_call x1, Pallas kernels: 30.4 us -> 25.1 us  [local(): pl.pallas_call(functools.partial(light_kernel, slabs, groups), out_shape=...]
where the time goes in v2:
time: 30.1 us; the launch traced here: 30 us
  Pallas kernels  29.3 us (97%)
  between operations  0.64 us (2%)
    pallas_call x1, Pallas kernels, local(): pl.pallas_call(functools.partial(light_kernel, slabs, groups), out_shape=...  25.1 us
    pallas_call x1, Pallas kernels, local(): pl.pallas_call(functools.partial(gradient_kernel, float(slices * slabs)),...  4.27 us

profile of v2, /device:TPU:4, one launch (start us, length us, event | category | flops | bytes accessed | tf_op | source)
XLA Modules:
  0.0 30.0 jit_solution(14689516084379437890)
XLA Ops:
  0.6 25.1 %light.1 = (f32[3,32,16,1024]{3,2,1,0:T(8,128)S(1)}, f32[32,16,1024]{2,1,0:T(8,128)S(1)}, f32[32,16,1024]{2,1,0:T(8,128)S(1)}, f32[32,16,1024]{2,1,0:T(8,128)S(1...) custom-call(bf16[32,16,1024]{2,1,0:T(8,128)(2,1)} %dens_hbm.1, ...), custom_call_target="tpu_custom_call" | custom-call | tf_op jit(solution)/shard_map/light/pallas_call | solution.py:530
  25.7 4.3 %gradient.1 = (f32[32,16,1024]{2,1,0:T(8,128)}, f32[3,32,16,1024]{3,2,1,0:T(8,128)}) custom-call(f32[3,32,16,1024]{3,2,1,0:T(8,128)S(1)} %get-tuple-element.9.colour_ref, f32[32,16,1024]{2,1,0:T(8,128)S(1)} %get-tuple-element.10.lit_ref, f32[32,16,1024]{2,1,0:T(8,128)S(1)} %get-tuple-element.11.through_ref, f32[32,16,1024]{2,1,0:T(8,128)S(1)} %get-tuple-element.12.slope_ref, ...), custom_call_target="tpu_custom_call" | custom-call | tf_op jit(solution)/shard_map/gradient/pallas_call | solution.py:569

commit v3 on v2

--- a/solution.py
+++ b/solution.py
@@ -85,7 +85,7 @@
     dens_hbm,
     colour_hbm,
     target_hbm,
-    rank_ref,
+    rank_hbm,
     colour_out,
     lit_out,
     through_out,
@@ -105,6 +105,9 @@
     answer_sent,
     answer_got,
     codes,
+    slice_got,
+    rank_ref,
+    rank_sem,
     dens_sem,
     colour_sem,
     target_sem,
@@ -135,10 +138,10 @@
         lanes = lanes_of(block)
         return (
             pltpu.make_async_copy(
-                dens_hbm.at[:, :, lanes], dens.at[pl.ds(1, slices), :, lanes], dens_sem.at[block]
+                dens_hbm.at[:, :, lanes], dens.at[block, pl.ds(1, slices)], dens_sem.at[block]
             ),
             pltpu.make_async_copy(
-                colour_hbm.at[:, :, :, lanes], colour_in.at[:, :, :, lanes], colour_sem.at[block]
+                colour_hbm.at[:, :, :, lanes], colour_in.at[block], colour_sem.at[block]
             ),
         )
 
@@ -148,29 +151,25 @@
     def owner_at(block, g):
         return lax.rem(my_band + far_first(g, bands), bands) * blocks + block
 
-    def start_inputs(k, _):
-        for copy in input_copies(block_at(k)):
-            copy.start()
-        return 0
-
-    lax.fori_loop(0, blocks, start_inputs, 0)
-    target_copy = pltpu.make_async_copy(
-        target_hbm.at[:, :, lanes_of(my_block)], target_in, target_sem
-    )
-    target_copy.start()
-
     barrier = pltpu.get_barrier_semaphore()
 
-    def greet(j, _):
-        pl.semaphore_signal(
-            barrier,
-            inc=1,
-            device_id={"depth": lax.rem(depth_at + j, slabs)},
-            device_id_type=pl.DeviceIdType.MESH,
-        )
-        return 0
-
-    lax.fori_loop(1, slabs, greet, 0)
+    def greet(k, _):
+        block = block_at(k)
+        for g in range(bands):
+            peer = owner_at(block, g)
+
+            @pl.when(peer != depth_at)
+            def _():
+                pl.semaphore_signal(
+                    barrier,
+                    inc=1,
+                    device_id={"depth": peer},
+                    device_id_type=pl.DeviceIdType.MESH,
+                )
+
+        return 0
+
+    lax.fori_loop(0, blocks, greet, 0)
     rows_up = lax.rem(rows_at + 1, groups)
     rows_down = lax.rem(rows_at + groups - 1, groups)
     depth_up = lax.rem(depth_at + 1, slabs)
@@ -180,12 +179,25 @@
             barrier, inc=1, device_id={"rows": peer}, device_id_type=pl.DeviceIdType.MESH
         )
 
+    def start_inputs(k, _):
+        for copy in input_copies(block_at(k)):
+            copy.start()
+        return 0
+
+    lax.fori_loop(0, blocks, start_inputs, 0)
+    target_copy = pltpu.make_async_copy(
+        target_hbm.at[:, :, lanes_of(my_block)], target_in, target_sem
+    )
+    target_copy.start()
+    rank_copy = pltpu.make_async_copy(rank_hbm, rank_ref, rank_sem)
+    rank_copy.start()
+
     slice_up = remote(
-        dens_hbm.at[slices - 1], dens.at[0], rim_send_sem.at[0], rim_recv_sem.at[0], "depth", depth_up
+        dens_hbm.at[slices - 1], slice_got.at[0], rim_send_sem.at[0], rim_recv_sem.at[0], "depth", depth_up
     )
     slice_down = remote(
         dens_hbm.at[0],
-        dens.at[slices + 1],
+        slice_got.at[1],
         rim_send_sem.at[1],
         rim_recv_sem.at[1],
         "depth",
@@ -208,6 +220,19 @@
             owner,
         )
 
+    def send_block(k, _):
+        block = block_at(k)
+        for g in range(bands):
+            owner = owner_at(block, g)
+
+            @pl.when(owner != depth_at)
+            def _():
+                partial_copy(owner).start()
+
+        return 0
+
+    send_from = jnp.where(my_block < blocks // 2, blocks - 1, 0)
+
     def forward_block(k, _):
         block = block_at(k)
         lanes = lanes_of(block)
@@ -219,7 +244,7 @@
             firsts, lasts = ([], [])
             for u in range(UNROLL):
                 z = step * UNROLL + u
-                x = dens[z + 1, :, lanes].astype(jnp.float32)
+                x = dens[block, z + 1].astype(jnp.float32)
                 firsts.append(x[:1])
                 lasts.append(x[rows - 1 :])
                 d = step_depth * jnp.log(1.0 + jnp.exp(x))
@@ -227,12 +252,12 @@
                 lit = light * opacity
                 blocked = blocked + lit
                 light = light - lit
-                lit_out[z, :, lanes] = lit
-                through_out[z, :, lanes] = light
+                lit_out[block, z] = lit
+                through_out[block, z] = light
                 for c in range(3):
-                    raw = colour_in[c, z, :, lanes].astype(jnp.float32)
+                    raw = colour_in[block, c, z].astype(jnp.float32)
                     colour = 1.0 / (1.0 + jnp.exp(-raw))
-                    colour_out[c, z, :, lanes] = colour
+                    colour_out[block, c, z] = colour
                     shine[c] = shine[c] + lit * colour
             chunk = pl.ds(pl.multiple_of(step * UNROLL, UNROLL), UNROLL)
             edge[0, chunk, lanes] = jnp.concatenate(firsts, axis=0)
@@ -245,8 +270,8 @@
         )
         mean = [value / blocked for value in shine]
         for c in range(3):
-            mean_out[c, :, lanes] = shine[c] + light * mean[c]
-        mean_out[3, :, lanes] = light
+            mean_out[block, c] = shine[c] + light * mean[c]
+        mean_out[block, 3] = light
         coded = [
             to_code((jnp.log(value) - middle) * scale)
             for value, (middle, scale) in zip((*mean, blocked), codings)
@@ -257,18 +282,16 @@
                 jnp.concatenate(packed, axis=0)
             )
 
-        @pl.when(k == 0)
+        @pl.when(k == send_from)
         def _():
             pl.semaphore_wait(barrier, slabs + 1)
+            lax.fori_loop(0, k, send_block, 0)
             slice_up.start()
             slice_down.start()
 
-        for g in range(bands):
-            owner = owner_at(block, g)
-
-            @pl.when(owner != depth_at)
-            def _():
-                partial_copy(owner).start()
+        @pl.when(k >= send_from)
+        def _():
+            send_block(k, 0)
 
         return 0
 
@@ -282,21 +305,22 @@
     ranks_column = jnp.zeros((slabs, LANES), jnp.int32)
     lane = lax.broadcasted_iota(jnp.int32, (slabs, LANES), 1)
     sub = lax.broadcasted_iota(jnp.int32, (slabs, LANES), 0)
+    rank_copy.wait()
     for s in range(slabs):
         rank = rank_ref[s]
-        ranks_row = jnp.where(lane == s, rank, ranks_row)
+        ranks_row = jnp.where(lane % slabs == s, rank, ranks_row)
         ranks_column = jnp.where(sub == s, rank, ranks_column)
-    earlier = (ranks_row < ranks_column).astype(jnp.float32)[:, :slabs]
-    later = (ranks_row > ranks_column).astype(jnp.float32)[:, :slabs]
+    thrice = 3 * slabs
+    earlier = (ranks_row < ranks_column).astype(jnp.bfloat16)[:, :thrice]
+    later = (ranks_row > ranks_column).astype(jnp.bfloat16)[:, :thrice]
 
     def slope_block(block, _):
-        lanes = lanes_of(block)
 
         def slope_step(step, _):
             for u in range(UNROLL):
                 z = step * UNROLL + u
-                x = dens[z + 1, :, lanes].astype(jnp.float32)
-                slope_out[z, :, lanes] = optical_depth / (1.0 + jnp.exp(-x))
+                x = dens[block, z + 1].astype(jnp.float32)
+                slope_out[block, z] = optical_depth / (1.0 + jnp.exp(-x))
             return 0
 
         return lax.fori_loop(0, slices // UNROLL, slope_step, 0)
@@ -320,11 +344,13 @@
         return from_log_code(coded, *codings[c])
 
     def mixed(matrix, value):
+        parts = []
+        for _ in range(3):
+            part = value.astype(jnp.bfloat16)
+            value = value - part.astype(jnp.float32)
+            parts.append(part)
         return jnp.dot(
-            matrix,
-            value,
-            precision=lax.Precision.HIGHEST,
-            preferred_element_type=jnp.float32,
+            matrix, jnp.concatenate(parts, axis=0), preferred_element_type=jnp.float32
         )
 
     blocked = gathered(3)
@@ -382,14 +408,6 @@
     for copy in (slice_up, slice_down, row_up, row_down):
         copy.wait()
 
-    @pl.when(depth_at == 0)
-    def _():
-        dens[0] = dens[1]
-
-    @pl.when(depth_at == slabs - 1)
-    def _():
-        dens[slices + 1] = dens[slices]
-
     rim[...] = rim_got[...].astype(jnp.float32)
 
     @pl.when(rows_at == 0)
@@ -410,18 +428,21 @@
             above, below = (rim[0, chunk, lanes], rim[1, chunk, lanes])
             for u in range(UNROLL):
                 z = step * UNROLL + u
-                high = dens[z + 2, :, lanes].astype(jnp.float32)
+                high = dens[block, z + 2].astype(jnp.float32)
                 upper = jnp.where(row == 0, above[u : u + 1], pltpu.roll(centre, 1, axis=0))
                 lower = jnp.where(
                     row == rows - 1, below[u : u + 1], pltpu.roll(centre, rows - 1, axis=0)
                 )
-                smooth_out[z, :, lanes] = (2.0 * smooth_weight) * (
+                smooth_out[block, z] = (2.0 * smooth_weight) * (
                     (centre - low) + (centre - high) + (centre - upper) + (centre - lower)
                 )
                 low, centre = centre, high
             return low, centre
 
-        start = (dens[0, :, lanes].astype(jnp.float32), dens[1, :, lanes].astype(jnp.float32))
+        first, last = (dens[block, 1], dens[block, slices])
+        dens[block, 0] = jnp.where(depth_at == 0, first, slice_got[0, :, lanes])
+        dens[block, slices + 1] = jnp.where(depth_at == slabs - 1, last, slice_got[1, :, lanes])
+        start = (dens[block, 0].astype(jnp.float32), first.astype(jnp.float32))
         lax.fori_loop(0, slices // UNROLL, smooth_step, start)
         return 0
 
@@ -449,8 +470,7 @@
     dens_sem,
     colour_sem,
 ):
-    slices, rows, width = lit_ref.shape
-    blocks = width // LANES
+    blocks, slices, rows, _ = lit_ref.shape
     bands = rows // BAND_ROWS
     message = 4 * BAND_ROWS
     band_rows = blocks * message
@@ -460,17 +480,16 @@
         lanes = pl.ds(pl.multiple_of(block * LANES, LANES), LANES)
         return (
             pltpu.make_async_copy(
-                dens_grad.at[:, :, lanes], dens_grad_hbm.at[:, :, lanes], dens_sem.at[block]
+                dens_grad.at[block], dens_grad_hbm.at[:, :, lanes], dens_sem.at[block]
             ),
             pltpu.make_async_copy(
-                colour_grad.at[:, :, :, lanes],
+                colour_grad.at[block],
                 colour_grad_hbm.at[:, :, :, lanes],
                 colour_sem.at[block],
             ),
         )
 
     def gradient_block(block, _):
-        lanes = pl.ds(pl.multiple_of(block * LANES, LANES), LANES)
         words = [
             as_floats(answer_ref[pl.ds(pl.multiple_of(g * band_rows + block * message, message), message), :])
             for g in range(bands)
@@ -481,24 +500,24 @@
             return from_answer_code(jnp.concatenate(coded, axis=0), scales[c])
 
         residual = [answer(c) for c in range(3)]
-        whole = mean_ref[3, :, lanes] * answer(3)
+        whole = mean_ref[block, 3] * answer(3)
         for c in range(3):
-            whole = whole + residual[c] * mean_ref[c, :, lanes]
+            whole = whole + residual[c] * mean_ref[block, c]
         strong = [slices_total * value for value in residual]
 
         def gradient_step(step, remaining):
             for u in range(UNROLL):
                 z = step * UNROLL + u
-                lit = lit_ref[z, :, lanes]
+                lit = lit_ref[block, z]
                 seen = jnp.zeros_like(lit)
                 for c in range(3):
-                    colour = colour_ref[c, z, :, lanes]
+                    colour = colour_ref[block, c, z]
                     seen = seen + residual[c] * colour
-                    colour_grad[c, z, :, lanes] = (strong[c] * lit) * (colour * (1.0 - colour))
+                    colour_grad[block, c, z] = (strong[c] * lit) * (colour * (1.0 - colour))
                 remaining = remaining - lit * seen
-                dens_grad[z, :, lanes] = (
-                    slope_ref[z, :, lanes] * (through_ref[z, :, lanes] * seen - remaining)
-                    + smooth_ref[z, :, lanes]
+                dens_grad[block, z] = (
+                    slope_ref[block, z] * (through_ref[block, z] * seen - remaining)
+                    + smooth_ref[block, z]
                 )
             return remaining
 
@@ -522,6 +541,8 @@
     blocks = width // LANES
     message = 4 * BAND_ROWS
     voxels = (slices, rows, width)
+    blocked = (blocks, slices, rows, LANES)
+    coloured = (blocks, 3, slices, rows, LANES)
     f32 = jnp.float32
     bf16 = jnp.bfloat16
     anywhere = pl.BlockSpec(memory_space=pl.ANY)
@@ -530,19 +551,19 @@
     saved = pl.pallas_call(
         functools.partial(light_kernel, slabs, groups),
         out_shape=(
-            pltpu.VMEM((3, *voxels), f32),
-            pltpu.VMEM(voxels, f32),
-            pltpu.VMEM(voxels, f32),
-            pltpu.VMEM(voxels, f32),
-            pltpu.VMEM(voxels, f32),
-            pltpu.VMEM((4, rows, width), f32),
+            pltpu.VMEM(coloured, f32),
+            pltpu.VMEM(blocked, f32),
+            pltpu.VMEM(blocked, f32),
+            pltpu.VMEM(blocked, f32),
+            pltpu.VMEM(blocked, f32),
+            pltpu.VMEM((blocks, 4, rows, LANES), f32),
             packet,
         ),
-        in_specs=[anywhere, anywhere, anywhere, pl.BlockSpec(memory_space=pltpu.SMEM)],
+        in_specs=[anywhere] * 4,
         out_specs=(vmem,) * 7,
         scratch_shapes=[
-            pltpu.VMEM((slices + 2, rows, width), bf16),
-            pltpu.VMEM((3, *voxels), bf16),
+            pltpu.VMEM((blocks, slices + 2, rows, LANES), bf16),
+            pltpu.VMEM(coloured, bf16),
             pltpu.VMEM((3, rows, LANES), f32),
             pltpu.VMEM((2, slices, width), f32),
             pltpu.VMEM((2, slices, width), bf16),
@@ -553,6 +574,9 @@
             packet,
             packet,
             pltpu.VMEM((slabs * message, LANES), f32),
+            pltpu.VMEM((2, rows, width), bf16),
+            pltpu.SMEM((slabs,), jnp.int32),
+            pltpu.SemaphoreType.DMA,
             pltpu.SemaphoreType.DMA((blocks,)),
             pltpu.SemaphoreType.DMA((blocks,)),
             pltpu.SemaphoreType.DMA,
@@ -575,8 +599,8 @@
         in_specs=[vmem] * 7,
         out_specs=(anywhere, anywhere),
         scratch_shapes=[
-            pltpu.VMEM(voxels, f32),
-            pltpu.VMEM((3, *voxels), f32),
+            pltpu.VMEM(blocked, f32),
+            pltpu.VMEM(coloured, f32),
             pltpu.SemaphoreType.DMA((blocks,)),
             pltpu.SemaphoreType.DMA((blocks,)),
         ],

time: 30.1 us -> 27.2 us (0.904)
  Pallas kernels: 29.3 us -> 26.5 us
    pallas_call x1, Pallas kernels: 25.1 us -> 22.8 us  [local(): pl.pallas_call(functools.partial(light_kernel, slabs, groups), out_shape=...]
    pallas_call x1, Pallas kernels: 4.27 us -> 3.66 us  [local(): pl.pallas_call(functools.partial(gradient_kernel, float(slices * slabs)),...]
where the time goes in v3:
time: 27.2 us; the launch traced here: 27.1 us
  Pallas kernels  26.5 us (97%)
  between operations  0.64 us (2%)
    pallas_call x1, Pallas kernels, local(): pl.pallas_call(functools.partial(light_kernel, slabs, groups), out_shape=...  22.8 us
    pallas_call x1, Pallas kernels, local(): pl.pallas_call(functools.partial(gradient_kernel, float(slices * slabs)),...  3.66 us

profile of v3, /device:TPU:4, one launch (start us, length us, event | category | flops | bytes accessed | tf_op | source)
XLA Modules:
  0.0 27.1 jit_solution(8146573567390027722)
XLA Ops:
  0.6 22.8 %light.1 = (f32[8,3,32,16,128]{4,3,2,1,0:T(8,128)S(1)}, f32[8,32,16,128]{3,2,1,0:T(8,128)S(1)}, f32[8,32,16,128]{3,2,1,0:T(8,128)S(1)}, f32[8,32,16,128]{3,2,1,0...) custom-call(bf16[32,16,1024]{2,1,0:T(8,128)(2,1)} %dens_hbm.1, ...), custom_call_target="tpu_custom_call" | custom-call | tf_op jit(solution)/shard_map/light/pallas_call | solution.py:551
  23.5 3.7 %gradient.1 = (f32[32,16,1024]{2,1,0:T(8,128)}, f32[3,32,16,1024]{3,2,1,0:T(8,128)}) custom-call(f32[8,3,32,16,128]{4,3,2,1,0:T(8,128)S(1)} %get-tuple-element.9.colour_ref, f32[8,32,16,128]{3,2,1,0:T(8,128)S(1)} %get-tuple-element.10.lit_ref, f32[8,32,16,128]{3,2,1,0:T(8,128)S(1)} %get-tuple-element.11.through_ref, ...), custom_call_target="tpu_custom_call" | custom-call | tf_op jit(solution)/shard_map/gradient/pallas_call | solution.py:593

commit v4 on v3

--- a/solution.py
+++ b/solution.py
@@ -448,10 +448,10 @@
 
     lax.fori_loop(0, blocks, smooth_block, 0)
 
+    pltpu.make_async_copy(partial_sent.at[others], partial_sent.at[others], send_sem.at[0]).wait()
+    pltpu.make_async_copy(answer_sent.at[others], answer_sent.at[others], send_sem.at[1]).wait()
     pltpu.make_async_copy(answer_got.at[others], answer_got.at[others], recv_sem.at[1]).wait()
     answer_out[...] = answer_got[...]
-    pltpu.make_async_copy(partial_sent.at[others], partial_sent.at[others], send_sem.at[0]).wait()
-    pltpu.make_async_copy(answer_sent.at[others], answer_sent.at[others], send_sem.at[1]).wait()
 
 
 def gradient_kernel(
@@ -476,15 +476,16 @@
     band_rows = blocks * message
     scales = answer_scales()
 
-    def output_copies(block):
+    def output_copies(block, start, count):
+        some = pl.ds(start, count)
         lanes = pl.ds(pl.multiple_of(block * LANES, LANES), LANES)
         return (
             pltpu.make_async_copy(
-                dens_grad.at[block], dens_grad_hbm.at[:, :, lanes], dens_sem.at[block]
+                dens_grad.at[block, some], dens_grad_hbm.at[some, :, lanes], dens_sem.at[block]
             ),
             pltpu.make_async_copy(
-                colour_grad.at[block],
-                colour_grad_hbm.at[:, :, :, lanes],
+                colour_grad.at[block, :, some],
+                colour_grad_hbm.at[:, some, :, lanes],
                 colour_sem.at[block],
             ),
         )
@@ -519,17 +520,17 @@
                     slope_ref[block, z] * (through_ref[block, z] * seen - remaining)
                     + smooth_ref[block, z]
                 )
+            for copy in output_copies(block, step * UNROLL, UNROLL):
+                copy.start()
             return remaining
 
         lax.fori_loop(0, slices // UNROLL, gradient_step, whole)
-        for copy in output_copies(block):
-            copy.start()
         return 0
 
     lax.fori_loop(0, blocks, gradient_block, 0)
 
     def finish(block, _):
-        for copy in output_copies(block):
+        for copy in output_copies(block, 0, slices):
             copy.wait()
         return 0
 

time: 27.2 us -> 27 us (level)
  no operation moved by 1% of the time
where the time goes in v4:
time: 27 us; the launch traced here: 26.9 us
  Pallas kernels  26.3 us (97%)
  between operations  0.64 us (2%)
    pallas_call x1, Pallas kernels, local(): pl.pallas_call(functools.partial(light_kernel, slabs, groups), out_shape=...  22.8 us
    pallas_call x1, Pallas kernels, local(): pl.pallas_call(functools.partial(gradient_kernel, float(slices * slabs)),...  3.45 us

profile of v4, /device:TPU:4, one launch (start us, length us, event | category | flops | bytes accessed | tf_op | source)
XLA Modules:
  0.0 26.9 jit_solution(3595185440815444565)
XLA Ops:
  0.6 22.8 %light.1 = (f32[8,3,32,16,128]{4,3,2,1,0:T(8,128)S(1)}, f32[8,32,16,128]{3,2,1,0:T(8,128)S(1)}, f32[8,32,16,128]{3,2,1,0:T(8,128)S(1)}, f32[8,32,16,128]{3,2,1,0...) custom-call(bf16[32,16,1024]{2,1,0:T(8,128)(2,1)} %dens_hbm.1, ...), custom_call_target="tpu_custom_call" | custom-call | tf_op jit(solution)/shard_map/light/pallas_call | solution.py:552
  23.5 3.5 %gradient.1 = (f32[32,16,1024]{2,1,0:T(8,128)}, f32[3,32,16,1024]{3,2,1,0:T(8,128)}) custom-call(f32[8,3,32,16,128]{4,3,2,1,0:T(8,128)S(1)} %get-tuple-element.9.colour_ref, f32[8,32,16,128]{3,2,1,0:T(8,128)S(1)} %get-tuple-element.10.lit_ref, f32[8,32,16,128]{3,2,1,0:T(8,128)S(1)} %get-tuple-element.11.through_ref, ...), custom_call_target="tpu_custom_call" | custom-call | tf_op jit(solution)/shard_map/gradient/pallas_call | solution.py:594

commit v5 on v4

--- a/solution.py
+++ b/solution.py
@@ -392,7 +392,8 @@
         )
 
     def answer_start(k, _):
-        block = block_at(k)
+        half = blocks // 2
+        block = lax.rem(my_block + k, half) + (k // half) * half
         for g in range(bands):
             slab = owner_at(block, g)
 

time: 27 us -> 27.1 us (level)
  no operation moved by 1% of the time
where the time goes in v5:
time: 27.1 us; the launch traced here: 27 us
  Pallas kernels  26.3 us (97%)
  between operations  0.64 us (2%)
    pallas_call x1, Pallas kernels, local(): pl.pallas_call(functools.partial(light_kernel, slabs, groups), out_shape=...  22.9 us
    pallas_call x1, Pallas kernels, local(): pl.pallas_call(functools.partial(gradient_kernel, float(slices * slabs)),...  3.45 us

profile of v5, /device:TPU:4, one launch (start us, length us, event | category | flops | bytes accessed | tf_op | source)
XLA Modules:
  0.0 27.0 jit_solution(6429219095642057320)
XLA Ops:
  0.6 22.9 %light.1 = (f32[8,3,32,16,128]{4,3,2,1,0:T(8,128)S(1)}, f32[8,32,16,128]{3,2,1,0:T(8,128)S(1)}, f32[8,32,16,128]{3,2,1,0:T(8,128)S(1)}, f32[8,32,16,128]{3,2,1,0...) custom-call(bf16[32,16,1024]{2,1,0:T(8,128)(2,1)} %dens_hbm.1, ...), custom_call_target="tpu_custom_call" | custom-call | tf_op jit(solution)/shard_map/light/pallas_call | solution.py:553
  23.5 3.5 %gradient.1 = (f32[32,16,1024]{2,1,0:T(8,128)}, f32[3,32,16,1024]{3,2,1,0:T(8,128)}) custom-call(f32[8,3,32,16,128]{4,3,2,1,0:T(8,128)S(1)} %get-tuple-element.9.colour_ref, f32[8,32,16,128]{3,2,1,0:T(8,128)S(1)} %get-tuple-element.10.lit_ref, f32[8,32,16,128]{3,2,1,0:T(8,128)S(1)} %get-tuple-element.11.through_ref, ...), custom_call_target="tpu_custom_call" | custom-call | tf_op jit(solution)/shard_map/gradient/pallas_call | solution.py:595
